TPU v7x, 128 devices: a whole 4x4x4 slice. The times are simulated.
128 devices in a mesh: replica: 16 (over z_hi, y, core), shard: 8 (over x, z_lo).
Axes of the slice: x: 4, y: 4, z: 4 (z_hi: 2, z_lo: 2; z = z_hi * 2 + z_lo), core: 2. Of those that a mesh axis runs over, the one named last changes fastest.
Arguments:
- student_ctx: bfloat16 [163840, 1536], P(('replica', 'shard')), may hold values from -24 to 24
- out_grad: bfloat16 [163840, 1536], P(('replica', 'shard')), may hold values from -0.015625 to 0.015625
- weight: float32 [1536, 1536], P('shard'), may hold values from -0.15625 to 0.15625
- moment_one: float32 [1536, 1536], P('shard'), may hold values from -6 to 6
- moment_two: float32 [1536, 1536], P('shard'), may hold values from 0.05 to 2
- teacher: float32 [1536, 1536], P('shard'), may hold values from -0.15625 to 0.15625
- teach_input: bfloat16 [65536, 1536], P(('replica', 'shard')), may hold values from -6 to 6
- teach_ctx: bfloat16 [65536, 1536], P(('replica', 'shard')), may hold values from -6 to 6
Outputs:
- ctx_grad: bfloat16 [163840, 1536], P(('replica', 'shard'))
- weight_next: float32 [1536, 1536], P('shard')
- moment_one_next: float32 [1536, 1536], P('shard')
- moment_two_next: float32 [1536, 1536], P('shard')
- teacher_next: float32 [1536, 1536], P('shard')
- teacher_out: bfloat16 [65536, 1536], P(('replica', 'shard'))
All inputs are finite; a program needn't handle non-finite values.
Results may differ from a plain program's by a relative error of at most 0.0043.
The roundings to bfloat16 on the way count: a program that leaves them out, or rounds other values in their place, can miss the bound.
Values may be sent and summed in bfloat16 or wider, within the bound.
A program may use at most 192 MiB of HBM per device.

v0:
```python
import jax
import jax.numpy as jnp
from jax import lax
from jax.sharding import PartitionSpec as P

STEP = 100
beta_one = 0.9
beta_two = 0.999
adam_eps = 1e-08
learn_rate = 0.001
decay_rate = 0.04
momentum = 0.994


def body(student_ctx, out_grad, weight, moment_one, moment_two, teacher, teach_input, teach_ctx):
    features = weight.shape[1]
    token_count = student_ctx.shape[0]
    weight_half = weight.astype(jnp.bfloat16)
    teacher_next = momentum * teacher + (1.0 - momentum) * weight
    teacher_half = teacher_next.astype(jnp.bfloat16)
    columns = teach_ctx
    projected = jnp.dot(
        columns,
        lax.all_gather(teacher_half, "shard", axis=0, tiled=True),
        preferred_element_type=jnp.float32,
    )
    teacher_out = (teach_input.astype(jnp.float32) + projected).astype(jnp.bfloat16)
    product = lax.dot_general(
        out_grad,
        lax.all_gather(weight_half, "shard", axis=0, tiled=True),
        (((1,), (1,)), ((), ())),
        preferred_element_type=jnp.float32,
    )
    ctx_grad = product.astype(jnp.bfloat16)
    n_copies = lax.axis_size("replica")
    n_groups = lax.axis_size("shard")
    block_rows = features // (n_copies * n_groups)
    virtual_ctx = student_ctx.reshape(token_count, n_groups, n_copies, block_rows)
    virtual_ctx = virtual_ctx.transpose(0, 2, 1, 3).reshape(token_count, features)
    columns = virtual_ctx
    own_block = lax.psum_scatter(
        lax.dot_general(
            columns, out_grad, (((0,), (0,)), ((), ())), preferred_element_type=jnp.float32
        ),
        ("replica", "shard"),
        scatter_dimension=0,
        tiled=True,
    )
    gradient = lax.all_gather(own_block.astype(jnp.bfloat16), "replica", axis=0, tiled=True).astype(
        own_block.dtype
    )
    moment_one_next = beta_one * moment_one + (1.0 - beta_one) * gradient
    moment_two_next = beta_two * moment_two + (1.0 - beta_two) * gradient * gradient
    correct_one = 1.0 - beta_one**STEP
    correct_two = 1.0 - beta_two**STEP
    update = (
        moment_one_next / correct_one / (jnp.sqrt(moment_two_next / correct_two) + adam_eps)
        + decay_rate * weight
    )
    weight_next = weight - learn_rate * update
    return (ctx_grad, weight_next, moment_one_next, moment_two_next, teacher_next, teacher_out)


def solution(mesh):
    return jax.shard_map(
        body,
        mesh=mesh,
        in_specs=(
            P(("replica", "shard"), None),
            P(("replica", "shard"), None),
            P("shard", None),
            P("shard", None),
            P("shard", None),
            P("shard", None),
            P(("replica", "shard"), None),
            P(("replica", "shard"), None),
        ),
        out_specs=(
            P(("replica", "shard"), None),
            P("shard", None),
            P("shard", None),
            P("shard", None),
            P("shard", None),
            P(("replica", "shard"), None),
        ),
        check_vma=False,
    )
```

profile of v0, /device:TPU:4, one launch (start us, length us, event | category | flops | bytes accessed | tf_op | source)
XLA Modules:
  0.0 783.4 jit_solution(11342597224027583799)
XLA Ops:
  7.2 6.4 copy.20
  13.6 6.9 reshape.18
  20.5 5.5 copy.21
  26.0 7.0 reshape.19
  33.0 11.5 %fusion.8 = f32[1536,1536]{1,0:T(8,128)} fusion(bf16[1280,1536]{0,1:T(8,128)(2,1)} %reshape.19, bf16[1280,1536]{1,0:T(8,128)(2,1)} %param.9), kind=kOutput, calls=%fused_computation.13 | convolution fusion | flops 6039797760 | bytes 17301504 | tf_op jit(solution)/shard_map/dot_general | solution.py:42
  44.5 367.8 %fusion = f32[16,1536]{1,0:T(8,128)S(1)} fusion(f32[1536,1536]{1,0:T(8,128)} %fusion.8), kind=kCustom, calls=%all-reduce-scatter | all-reduce-scatter fusion | flops 3145729 | bytes 9535488
  412.3 1.3 collective-permute-start.30
  413.6 1.3 collective-permute-start.31
  414.9 1.3 collective-permute-start.29
  416.2 14.3 %collective-permute-start.28 = (bf16[16,1536]{1,0:T(8,128)(2,1)S(1)}, bf16[16,1536]{1,0:T(8,128)(2,1)S(1)}, u32[]{:S(2)}, u32[]{:S(2)}) collective-permute-start(bf16[16,1536]{1,0:T(8,128)(2,1)S(1)} %convert.62), channel_id=1, source_target_pairs={{0,29},{1,30},{2,31},{3,32},{4,33},{5,34},{6,35},{7,36},{8,37},{9,... | collective-permute-start | bytes 147464
  430.5 1.3 collective-permute-start.27
  431.8 1.3 collective-permute-start.26
  433.1 1.3 collective-permute-start.25
  434.5 1.3 collective-permute-start.24
  435.8 1.3 collective-permute-start.23
  437.1 1.3 collective-permute-start.22
  438.4 8.7 %collective-permute-start.21 = (bf16[16,1536]{1,0:T(8,128)(2,1)S(1)}, bf16[16,1536]{1,0:T(8,128)(2,1)S(1)}, u32[]{:S(2)}, u32[]{:S(2)}) collective-permute-start(bf16[16,1536]{1,0:T(8,128)(2,1)S(1)} %convert.62), channel_id=1, source_target_pairs={{0,22},{1,23},{2,24},{3,25},{4,26},{5,27},{6,28},{7,29},{8,30},{9,... | collective-permute-start | bytes 147464
  447.1 4.8 collective-permute-start.20
  451.9 4.5 collective-permute-start.19
  456.4 1.5 collective-permute-start.18
  458.0 2.2 collective-permute-start.17
  460.2 1.3 collective-permute-start.16
  461.6 2.2 collective-permute-start.15
  463.8 3.5 collective-permute-start.14
  467.3 1.6 collective-permute-start.13
  469.0 4.0 collective-permute-start.12
  473.0 2.2 collective-permute-start.11
  475.3 2.8 collective-permute-start.10
  478.1 3.6 collective-permute-start.9
  481.7 1.4 collective-permute-start.8
  483.2 2.5 collective-permute-start.7
  485.7 2.5 collective-permute-start.6
  488.3 2.7 collective-permute-start.5
  491.0 4.0 collective-permute-start.4
  495.0 1.9 collective-permute-start.3
  497.0 4.2 collective-permute-start.2
  501.3 3.4 collective-permute-start.1
  504.7 2.4 collective-permute-start
  508.4 3.2 collective-permute-done
  511.7 25.9 %concatenate = bf16[524,1536]{1,0:T(8,128)(2,1)S(1)} concatenate(bf16[12,1536]{1,0:T(8,128)(2,1)S(1)} %collective-permute-done.31, bf16[16,1536]{1,0:T(8,128)(2,1)S(1)} %collective-permute-done.30, bf16[16,1536]{1,0:T(8,128)(2,1)S(1)} %collective-permute-done.29, bf16[16,1536]{1,0:T(8,128)(2,1)S(1)} %collective-permute-done.28, bf16[16,1536]{1,0:T(8,128)(2,1)S(1)} %collective-permute-done.27, ...), dimensions={0} | concatenate | bytes 3268608
  537.7 21.4 %all-gather = bf16[16,12,1536]{2,1,0:T(8,128)(2,1)S(1)} all-gather(bf16[1,12,1536]{2,1,0:T(8,128)(2,1)S(1)} %fusion.4), channel_id=1, replica_groups=mesh['replica'=16,'shard'=8] {'replica'}, dimensions={0}, use_global_device_ids=true | all-gather | bytes 626688 | tf_op jit(solution)/shard_map/all_gather | solution.py:49
  559.2 5.6 fusion.5
  565.6 1.7 copy.22
  567.3 96.4 %all-gather.6.cloned.1.call-done = bf16[1536,1536]{1,0:T(8,128)(2,1)} async-done(((bf16[192,1536]{1,0:T(8,128)(2,1)}), bf16[1536,1536]{1,0:T(8,128)(2,1)}) %all-gather.6.cloned.1.call-update) | async-done | bytes 4718608 | tf_op jit(solution)/shard_map/all_gather | solution.py:24
  663.7 6.1 fusion.2
  669.8 2.6 copy.23
  672.4 93.5 %all-gather.4.cloned.1.call-done = bf16[1536,1536]{1,0:T(8,128)(2,1)} async-done(((bf16[192,1536]{1,0:T(8,128)(2,1)}), bf16[1536,1536]{1,0:T(8,128)(2,1)}) %all-gather.4.cloned.1.call-update) | async-done | bytes 4718608 | tf_op jit(solution)/shard_map/all_gather | solution.py:30
  765.9 10.6 %convolution_convert_fusion = bf16[1280,1536]{1,0:T(8,128)(2,1)} fusion(bf16[1280,1536]{1,0:T(8,128)(2,1)} %param.9, bf16[1536,1536]{1,0:T(8,128)(2,1)} %all-gather.4.cloned.1.call-done), kind=kOutput, calls=%fused_computation | convolution fusion | flops 6041763840 | bytes 12582912 | tf_op jit(solution)/shard_map/dot_general | solution.py:28
  (93 shorter events, 2.2 us)
Async XLA Ops:
  7.2 656.5 %copy-start = (bf16[512,1536]{1,0:T(8,128)(2,1)S(1)}, bf16[512,1536]{1,0:T(8,128)(2,1)}, u32[]{:S(2)}) copy-start(bf16[512,1536]{1,0:T(8,128)(2,1)} %param.15) | copy-start | bytes 4718596
  7.2 656.5 %all-gather.6.cloned.1.call-start = ((), (), s32[]{:S(2)}) async-start(), calls=%async_computation.1 | async-start | bytes 5308416 | tf_op jit(solution)/shard_map/all_gather | solution.py:24
  412.3 20.8 %collective-permute-start.30 = (bf16[16,1536]{1,0:T(8,128)(2,1)S(1)}, bf16[16,1536]{1,0:T(8,128)(2,1)S(1)}, u32[]{:S(2)}, u32[]{:S(2)}) collective-permute-start(bf16[16,1536]{1,0:T(8,128)(2,1)S(1)} %convert.62), channel_id=1, source_target_pairs={{0,31},{1,32},{2,33},{3,34},{4,35},{5,36},{6,37},{7,38},{8,39},{9,... | collective-permute-start | bytes 147464
  413.6 18.2 %collective-permute-start.31 = (bf16[12,1536]{1,0:T(8,128)(2,1)S(1)}, bf16[12,1536]{1,0:T(8,128)(2,1)S(1)}, u32[]{:S(2)}, u32[]{:S(2)}) collective-permute-start(bf16[12,1536]{1,0:T(8,128)(2,1)S(1)} %slice), channel_id=1, source_target_pairs={{0,32},{1,33},{2,34},{3,35},{4,36},{5,37},{6,38},{7,39},{8,40},{9,... | collective-permute-start | bytes 110600
  414.9 19.5 %collective-permute-start.29 = (bf16[16,1536]{1,0:T(8,128)(2,1)S(1)}, bf16[16,1536]{1,0:T(8,128)(2,1)S(1)}, u32[]{:S(2)}, u32[]{:S(2)}) collective-permute-start(bf16[16,1536]{1,0:T(8,128)(2,1)S(1)} %convert.62), channel_id=1, source_target_pairs={{0,30},{1,31},{2,32},{3,33},{4,34},{5,35},{6,36},{7,37},{8,38},{9,... | collective-permute-start | bytes 147464
  416.2 19.5 %collective-permute-start.28 = (bf16[16,1536]{1,0:T(8,128)(2,1)S(1)}, bf16[16,1536]{1,0:T(8,128)(2,1)S(1)}, u32[]{:S(2)}, u32[]{:S(2)}) collective-permute-start(bf16[16,1536]{1,0:T(8,128)(2,1)S(1)} %convert.62), channel_id=1, source_target_pairs={{0,29},{1,30},{2,31},{3,32},{4,33},{5,34},{6,35},{7,36},{8,37},{9,... | collective-permute-start | bytes 147464
  430.5 6.5 collective-permute-start.27
  431.8 6.5 collective-permute-start.26
  433.1 13.9 %collective-permute-start.25 = (bf16[16,1536]{1,0:T(8,128)(2,1)S(1)}, bf16[16,1536]{1,0:T(8,128)(2,1)S(1)}, u32[]{:S(2)}, u32[]{:S(2)}) collective-permute-start(bf16[16,1536]{1,0:T(8,128)(2,1)S(1)} %convert.62), channel_id=1, source_target_pairs={{0,26},{1,27},{2,28},{3,29},{4,30},{5,31},{6,32},{7,33},{8,34},{9,... | collective-permute-start | bytes 147464
  434.5 17.4 %collective-permute-start.24 = (bf16[16,1536]{1,0:T(8,128)(2,1)S(1)}, bf16[16,1536]{1,0:T(8,128)(2,1)S(1)}, u32[]{:S(2)}, u32[]{:S(2)}) collective-permute-start(bf16[16,1536]{1,0:T(8,128)(2,1)S(1)} %convert.62), channel_id=1, source_target_pairs={{0,25},{1,26},{2,27},{3,28},{4,29},{5,30},{6,31},{7,32},{8,33},{9,... | collective-permute-start | bytes 147464
  435.8 20.7 %collective-permute-start.23 = (bf16[16,1536]{1,0:T(8,128)(2,1)S(1)}, bf16[16,1536]{1,0:T(8,128)(2,1)S(1)}, u32[]{:S(2)}, u32[]{:S(2)}) collective-permute-start(bf16[16,1536]{1,0:T(8,128)(2,1)S(1)} %convert.62), channel_id=1, source_target_pairs={{0,24},{1,25},{2,26},{3,27},{4,28},{5,29},{6,30},{7,31},{8,32},{9,... | collective-permute-start | bytes 147464
  437.1 20.9 %collective-permute-start.22 = (bf16[16,1536]{1,0:T(8,128)(2,1)S(1)}, bf16[16,1536]{1,0:T(8,128)(2,1)S(1)}, u32[]{:S(2)}, u32[]{:S(2)}) collective-permute-start(bf16[16,1536]{1,0:T(8,128)(2,1)S(1)} %convert.62), channel_id=1, source_target_pairs={{0,23},{1,24},{2,25},{3,26},{4,27},{5,28},{6,29},{7,30},{8,31},{9,... | collective-permute-start | bytes 147464
  438.4 68.8 %copy-start.1 = (bf16[16,1536]{1,0:T(8,128)(2,1)}, bf16[16,1536]{1,0:T(8,128)(2,1)S(1)}, u32[]{:S(2)}) copy-start(bf16[16,1536]{1,0:T(8,128)(2,1)S(1)} %collective-permute-done.26) | copy-start | bytes 147460
  438.4 21.8 %collective-permute-start.21 = (bf16[16,1536]{1,0:T(8,128)(2,1)S(1)}, bf16[16,1536]{1,0:T(8,128)(2,1)S(1)}, u32[]{:S(2)}, u32[]{:S(2)}) collective-permute-start(bf16[16,1536]{1,0:T(8,128)(2,1)S(1)} %convert.62), channel_id=1, source_target_pairs={{0,22},{1,23},{2,24},{3,25},{4,26},{5,27},{6,28},{7,29},{8,30},{9,... | collective-permute-start | bytes 147464
  447.1 60.1 %copy-start.2 = (bf16[16,1536]{1,0:T(8,128)(2,1)}, bf16[16,1536]{1,0:T(8,128)(2,1)S(1)}, u32[]{:S(2)}) copy-start(bf16[16,1536]{1,0:T(8,128)(2,1)S(1)} %collective-permute-done.25) | copy-start | bytes 147460
  447.1 14.4 %collective-permute-start.20 = (bf16[16,1536]{1,0:T(8,128)(2,1)S(1)}, bf16[16,1536]{1,0:T(8,128)(2,1)S(1)}, u32[]{:S(2)}, u32[]{:S(2)}) collective-permute-start(bf16[16,1536]{1,0:T(8,128)(2,1)S(1)} %convert.62), channel_id=1, source_target_pairs={{0,21},{1,22},{2,23},{3,24},{4,25},{5,26},{6,27},{7,28},{8,29},{9,... | collective-permute-start | bytes 147464
  451.9 55.3 %copy-start.3 = (bf16[16,1536]{1,0:T(8,128)(2,1)}, bf16[16,1536]{1,0:T(8,128)(2,1)S(1)}, u32[]{:S(2)}) copy-start(bf16[16,1536]{1,0:T(8,128)(2,1)S(1)} %collective-permute-done.24) | copy-start | bytes 147460
  451.9 11.9 %collective-permute-start.19 = (bf16[16,1536]{1,0:T(8,128)(2,1)S(1)}, bf16[16,1536]{1,0:T(8,128)(2,1)S(1)}, u32[]{:S(2)}, u32[]{:S(2)}) collective-permute-start(bf16[16,1536]{1,0:T(8,128)(2,1)S(1)} %convert.62), channel_id=1, source_target_pairs={{0,20},{1,21},{2,22},{3,23},{4,24},{5,25},{6,26},{7,27},{8,28},{9,... | collective-permute-start | bytes 147464
  456.4 50.8 %copy-start.4 = (bf16[16,1536]{1,0:T(8,128)(2,1)}, bf16[16,1536]{1,0:T(8,128)(2,1)S(1)}, u32[]{:S(2)}) copy-start(bf16[16,1536]{1,0:T(8,128)(2,1)S(1)} %collective-permute-done.23) | copy-start | bytes 147460
  456.4 10.9 %collective-permute-start.18 = (bf16[16,1536]{1,0:T(8,128)(2,1)S(1)}, bf16[16,1536]{1,0:T(8,128)(2,1)S(1)}, u32[]{:S(2)}, u32[]{:S(2)}) collective-permute-start(bf16[16,1536]{1,0:T(8,128)(2,1)S(1)} %convert.62), channel_id=1, source_target_pairs={{0,19},{1,20},{2,21},{3,22},{4,23},{5,24},{6,25},{7,26},{8,27},{9,... | collective-permute-start | bytes 147464
  458.0 49.3 %copy-start.5 = (bf16[16,1536]{1,0:T(8,128)(2,1)}, bf16[16,1536]{1,0:T(8,128)(2,1)S(1)}, u32[]{:S(2)}) copy-start(bf16[16,1536]{1,0:T(8,128)(2,1)S(1)} %collective-permute-done.22) | copy-start | bytes 147460
  458.0 11.0 %collective-permute-start.17 = (bf16[16,1536]{1,0:T(8,128)(2,1)S(1)}, bf16[16,1536]{1,0:T(8,128)(2,1)S(1)}, u32[]{:S(2)}, u32[]{:S(2)}) collective-permute-start(bf16[16,1536]{1,0:T(8,128)(2,1)S(1)} %convert.62), channel_id=1, source_target_pairs={{0,18},{1,19},{2,20},{3,21},{4,22},{5,23},{6,24},{7,25},{8,26},{9,... | collective-permute-start | bytes 147464
  460.2 47.1 %copy-start.6 = (bf16[16,1536]{1,0:T(8,128)(2,1)}, bf16[16,1536]{1,0:T(8,128)(2,1)S(1)}, u32[]{:S(2)}) copy-start(bf16[16,1536]{1,0:T(8,128)(2,1)S(1)} %collective-permute-done.21) | copy-start | bytes 147460
  460.2 12.8 %collective-permute-start.16 = (bf16[16,1536]{1,0:T(8,128)(2,1)S(1)}, bf16[16,1536]{1,0:T(8,128)(2,1)S(1)}, u32[]{:S(2)}, u32[]{:S(2)}) collective-permute-start(bf16[16,1536]{1,0:T(8,128)(2,1)S(1)} %convert.62), channel_id=1, source_target_pairs={{0,17},{1,18},{2,19},{3,20},{4,21},{5,22},{6,23},{7,24},{8,25},{9,... | collective-permute-start | bytes 147464
  461.6 45.7 %copy-start.7 = (bf16[16,1536]{1,0:T(8,128)(2,1)}, bf16[16,1536]{1,0:T(8,128)(2,1)S(1)}, u32[]{:S(2)}) copy-start(bf16[16,1536]{1,0:T(8,128)(2,1)S(1)} %collective-permute-done.20) | copy-start | bytes 147460
  461.6 13.7 %collective-permute-start.15 = (bf16[16,1536]{1,0:T(8,128)(2,1)S(1)}, bf16[16,1536]{1,0:T(8,128)(2,1)S(1)}, u32[]{:S(2)}, u32[]{:S(2)}) collective-permute-start(bf16[16,1536]{1,0:T(8,128)(2,1)S(1)} %convert.62), channel_id=1, source_target_pairs={{0,16},{1,17},{2,18},{3,19},{4,20},{5,21},{6,22},{7,23},{8,24},{9,... | collective-permute-start | bytes 147464
  463.8 43.5 %copy-start.8 = (bf16[16,1536]{1,0:T(8,128)(2,1)}, bf16[16,1536]{1,0:T(8,128)(2,1)S(1)}, u32[]{:S(2)}) copy-start(bf16[16,1536]{1,0:T(8,128)(2,1)S(1)} %collective-permute-done.19) | copy-start | bytes 147460
  463.8 14.3 %collective-permute-start.14 = (bf16[16,1536]{1,0:T(8,128)(2,1)S(1)}, bf16[16,1536]{1,0:T(8,128)(2,1)S(1)}, u32[]{:S(2)}, u32[]{:S(2)}) collective-permute-start(bf16[16,1536]{1,0:T(8,128)(2,1)S(1)} %convert.62), channel_id=1, source_target_pairs={{0,15},{1,16},{2,17},{3,18},{4,19},{5,20},{6,21},{7,22},{8,23},{9,... | collective-permute-start | bytes 147464
  467.3 40.0 %copy-start.9 = (bf16[16,1536]{1,0:T(8,128)(2,1)}, bf16[16,1536]{1,0:T(8,128)(2,1)S(1)}, u32[]{:S(2)}) copy-start(bf16[16,1536]{1,0:T(8,128)(2,1)S(1)} %collective-permute-done.18) | copy-start | bytes 147460
  467.3 14.4 %collective-permute-start.13 = (bf16[16,1536]{1,0:T(8,128)(2,1)S(1)}, bf16[16,1536]{1,0:T(8,128)(2,1)S(1)}, u32[]{:S(2)}, u32[]{:S(2)}) collective-permute-start(bf16[16,1536]{1,0:T(8,128)(2,1)S(1)} %convert.62), channel_id=1, source_target_pairs={{0,14},{1,15},{2,16},{3,17},{4,18},{5,19},{6,20},{7,21},{8,22},{9,... | collective-permute-start | bytes 147464
  469.0 38.3 %copy-start.10 = (bf16[16,1536]{1,0:T(8,128)(2,1)}, bf16[16,1536]{1,0:T(8,128)(2,1)S(1)}, u32[]{:S(2)}) copy-start(bf16[16,1536]{1,0:T(8,128)(2,1)S(1)} %collective-permute-done.17) | copy-start | bytes 147460
  469.0 14.1 %collective-permute-start.12 = (bf16[16,1536]{1,0:T(8,128)(2,1)S(1)}, bf16[16,1536]{1,0:T(8,128)(2,1)S(1)}, u32[]{:S(2)}, u32[]{:S(2)}) collective-permute-start(bf16[16,1536]{1,0:T(8,128)(2,1)S(1)} %convert.62), channel_id=1, source_target_pairs={{0,13},{1,14},{2,15},{3,16},{4,17},{5,18},{6,19},{7,20},{8,21},{9,... | collective-permute-start | bytes 147464
  473.0 34.3 %copy-start.11 = (bf16[16,1536]{1,0:T(8,128)(2,1)}, bf16[16,1536]{1,0:T(8,128)(2,1)S(1)}, u32[]{:S(2)}) copy-start(bf16[16,1536]{1,0:T(8,128)(2,1)S(1)} %collective-permute-done.16) | copy-start | bytes 147460
  473.0 12.7 %collective-permute-start.11 = (bf16[16,1536]{1,0:T(8,128)(2,1)S(1)}, bf16[16,1536]{1,0:T(8,128)(2,1)S(1)}, u32[]{:S(2)}, u32[]{:S(2)}) collective-permute-start(bf16[16,1536]{1,0:T(8,128)(2,1)S(1)} %convert.62), channel_id=1, source_target_pairs={{0,12},{1,13},{2,14},{3,15},{4,16},{5,17},{6,18},{7,19},{8,20},{9,... | collective-permute-start | bytes 147464
  475.3 32.1 %copy-start.12 = (bf16[16,1536]{1,0:T(8,128)(2,1)}, bf16[16,1536]{1,0:T(8,128)(2,1)S(1)}, u32[]{:S(2)}) copy-start(bf16[16,1536]{1,0:T(8,128)(2,1)S(1)} %collective-permute-done.15) | copy-start | bytes 147460
  475.3 13.0 %collective-permute-start.10 = (bf16[16,1536]{1,0:T(8,128)(2,1)S(1)}, bf16[16,1536]{1,0:T(8,128)(2,1)S(1)}, u32[]{:S(2)}, u32[]{:S(2)}) collective-permute-start(bf16[16,1536]{1,0:T(8,128)(2,1)S(1)} %convert.62), channel_id=1, source_target_pairs={{0,11},{1,12},{2,13},{3,14},{4,15},{5,16},{6,17},{7,18},{8,19},{9,... | collective-permute-start | bytes 147464
  478.1 29.3 %copy-start.13 = (bf16[16,1536]{1,0:T(8,128)(2,1)}, bf16[16,1536]{1,0:T(8,128)(2,1)S(1)}, u32[]{:S(2)}) copy-start(bf16[16,1536]{1,0:T(8,128)(2,1)S(1)} %collective-permute-done.14) | copy-start | bytes 147460
  478.1 12.9 %collective-permute-start.9 = (bf16[16,1536]{1,0:T(8,128)(2,1)S(1)}, bf16[16,1536]{1,0:T(8,128)(2,1)S(1)}, u32[]{:S(2)}, u32[]{:S(2)}) collective-permute-start(bf16[16,1536]{1,0:T(8,128)(2,1)S(1)} %convert.62), channel_id=1, source_target_pairs={{0,10},{1,11},{2,12},{3,13},{4,14},{5,15},{6,16},{7,17},{8,18},{9,... | collective-permute-start | bytes 147464
  481.7 13.3 %collective-permute-start.8 = (bf16[16,1536]{1,0:T(8,128)(2,1)S(1)}, bf16[16,1536]{1,0:T(8,128)(2,1)S(1)}, u32[]{:S(2)}, u32[]{:S(2)}) collective-permute-start(bf16[16,1536]{1,0:T(8,128)(2,1)S(1)} %convert.62), channel_id=1, source_target_pairs={{0,9},{1,10},{2,11},{3,12},{4,13},{5,14},{6,15},{7,16},{8,17},{9,1... | collective-permute-start | bytes 147464
  483.2 13.8 %collective-permute-start.7 = (bf16[16,1536]{1,0:T(8,128)(2,1)S(1)}, bf16[16,1536]{1,0:T(8,128)(2,1)S(1)}, u32[]{:S(2)}, u32[]{:S(2)}) collective-permute-start(bf16[16,1536]{1,0:T(8,128)(2,1)S(1)} %convert.62), channel_id=1, source_target_pairs={{0,8},{1,9},{2,10},{3,11},{4,12},{5,13},{6,14},{7,15},{8,16},{9,17... | collective-permute-start | bytes 147464
  485.7 15.5 %collective-permute-start.6 = (bf16[16,1536]{1,0:T(8,128)(2,1)S(1)}, bf16[16,1536]{1,0:T(8,128)(2,1)S(1)}, u32[]{:S(2)}, u32[]{:S(2)}) collective-permute-start(bf16[16,1536]{1,0:T(8,128)(2,1)S(1)} %convert.62), channel_id=1, source_target_pairs={{0,7},{1,8},{2,9},{3,10},{4,11},{5,12},{6,13},{7,14},{8,15},{9,16}... | collective-permute-start | bytes 147464
  488.3 16.4 %collective-permute-start.5 = (bf16[16,1536]{1,0:T(8,128)(2,1)S(1)}, bf16[16,1536]{1,0:T(8,128)(2,1)S(1)}, u32[]{:S(2)}, u32[]{:S(2)}) collective-permute-start(bf16[16,1536]{1,0:T(8,128)(2,1)S(1)} %convert.62), channel_id=1, source_target_pairs={{0,6},{1,7},{2,8},{3,9},{4,10},{5,11},{6,12},{7,13},{8,14},{9,15},... | collective-permute-start | bytes 147464
  491.0 16.2 %collective-permute-start.4 = (bf16[16,1536]{1,0:T(8,128)(2,1)S(1)}, bf16[16,1536]{1,0:T(8,128)(2,1)S(1)}, u32[]{:S(2)}, u32[]{:S(2)}) collective-permute-start(bf16[16,1536]{1,0:T(8,128)(2,1)S(1)} %convert.62), channel_id=1, source_target_pairs={{0,5},{1,6},{2,7},{3,8},{4,9},{5,10},{6,11},{7,12},{8,13},{9,14},{... | collective-permute-start | bytes 147464
  495.0 12.2 %collective-permute-start.3 = (bf16[16,1536]{1,0:T(8,128)(2,1)S(1)}, bf16[16,1536]{1,0:T(8,128)(2,1)S(1)}, u32[]{:S(2)}, u32[]{:S(2)}) collective-permute-start(bf16[16,1536]{1,0:T(8,128)(2,1)S(1)} %convert.62), channel_id=1, source_target_pairs={{0,4},{1,5},{2,6},{3,7},{4,8},{5,9},{6,10},{7,11},{8,12},{9,13},{1... | collective-permute-start | bytes 147464
  497.0 10.2 %collective-permute-start.2 = (bf16[16,1536]{1,0:T(8,128)(2,1)S(1)}, bf16[16,1536]{1,0:T(8,128)(2,1)S(1)}, u32[]{:S(2)}, u32[]{:S(2)}) collective-permute-start(bf16[16,1536]{1,0:T(8,128)(2,1)S(1)} %convert.62), channel_id=1, source_target_pairs={{0,3},{1,4},{2,5},{3,6},{4,7},{5,8},{6,9},{7,10},{8,11},{9,12},{10... | collective-permute-start | bytes 147464
  501.3 6.0 collective-permute-start.1
  504.7 7.0 collective-permute-start
  564.8 201.1 %all-gather.4.cloned.1.call-start = ((), (), s32[]{:S(2)}) async-start(), calls=%async_computation | async-start | bytes 5308416 | tf_op jit(solution)/shard_map/all_gather | solution.py:30
  (13 other events, 141.3 us)
Sparse Core Ops, SparseCore 0:
  564.9 98.6 all-gather.5
  665.3 100.5 all-gather.3
where the time goes:
time: 786 us; the launch traced here: 783 us
  blocking collectives  389 us (49%)
  waiting for transfers between devices  194 us (25%)
  starting transfers between devices  94.3 us (12%)
  local copies, waits for them, and re-layouts  57.3 us (7%)
  matrix products  28.3 us (4%)
  between operations  15 us (2%)
    unnamed x1, blocking collectives  368 us
    all_gather x1, waiting for transfers between devices, body(): lax.all_gather(teacher_half, 'shard', axis=0, tiled=True)  96.4 us
    unnamed x32, starting transfers between devices  94.1 us
    all_gather x1, waiting for transfers between devices, body(): lax.all_gather(weight_half, 'shard', axis=0, tiled=True)  93.5 us
    unnamed x60, local copies, waits for them, and re-layouts  37.8 us
    all_gather x1, blocking collectives, body(): lax.all_gather(own_block.astype(jnp.bfloat16), 'replica', axis=0, tiled=T...  21.4 us
  transfers between devices with their start and end apart: 34, of which 3 were waited for; matrix products, arithmetic and copies ran while one was open for 1% of the time, Pallas kernels for 0%

commit v1 on v0

--- a/solution.py
+++ b/solution.py
@@ -21,7 +21,10 @@
     columns = teach_ctx
     projected = jnp.dot(
         columns,
-        lax.all_gather(teacher_half, "shard", axis=0, tiled=True),
+        jnp.concatenate(
+            lax.all_to_all(jnp.stack([teacher_half] * lax.axis_size("shard")), "shard", 0, 0),
+            axis=0,
+        ),
         preferred_element_type=jnp.float32,
     )
     teacher_out = (teach_input.astype(jnp.float32) + projected).astype(jnp.bfloat16)

time: 786 us -> 733 us (0.933)
  waiting for transfers between devices: 194 us -> 133 us
    all_gather x1 -> x0, waiting for transfers between devices: 96.4 us -> none  [body(): lax.all_gather(teacher_half, 'shard', axis=0, tiled=True)]
    all_to_all x0 -> x1, waiting for transfers between devices: none -> 75.6 us  [body(): lax.all_to_all(jnp.stack([teacher_half] * lax.axis_size('shard')), 'shard...]
    all_gather x1, waiting for transfers between devices: 93.5 us -> 55.2 us  [body(): lax.all_gather(weight_half, 'shard', axis=0, tiled=True)]
    all_to_all x0 -> x1, starting transfers between devices: none -> 7.96 us  [body(): lax.all_to_all(jnp.stack([teacher_half] * lax.axis_size('shard')), 'shard...]
    unnamed x60 -> x62, local copies, waits for them, and re-layouts: 37.8 us -> 36.6 us
  transfers between devices with their start and end apart: 34 -> 34, of which waited for: 3 -> 3; matrix products, arithmetic and copies ran while one was open for 1% -> 2% of each run, Pallas kernels for 0% -> 0%
where the time goes in v1:
time: 733 us; the launch traced here: 730 us
  blocking collectives  391 us (53%)
  waiting for transfers between devices  133 us (18%)
  starting transfers between devices  99.4 us (14%)
  local copies, waits for them, and re-layouts  58.7 us (8%)
  matrix products  27.7 us (4%)
  between operations  14.9 us (2%)
    unnamed x1, blocking collectives  368 us
    unnamed x32, starting transfers between devices  91.4 us
    all_to_all x1, waiting for transfers between devices, body(): lax.all_to_all(jnp.stack([teacher_half] * lax.axis_size('shard')), 'shard...  75.6 us
    all_gather x1, waiting for transfers between devices, body(): lax.all_gather(weight_half, 'shard', axis=0, tiled=True)  55.2 us
    unnamed x62, local copies, waits for them, and re-layouts  36.6 us
    all_gather x1, blocking collectives, body(): lax.all_gather(own_block.astype(jnp.bfloat16), 'replica', axis=0, tiled=T...  22.5 us
  transfers between devices with their start and end apart: 34, of which 3 were waited for; matrix products, arithmetic and copies ran while one was open for 2% of the time, Pallas kernels for 0%

profile of v1, /device:TPU:4, one launch (start us, length us, event | category | flops | bytes accessed | tf_op | source)
XLA Modules:
  0.0 729.9 jit_solution(10619389782958326323)
XLA Ops:
  7.2 6.4 copy.20
  13.6 6.9 reshape.23
  20.5 5.5 copy.21
  26.0 7.0 reshape.24
  33.0 11.5 %fusion.8 = f32[1536,1536]{1,0:T(8,128)} fusion(bf16[1280,1536]{0,1:T(8,128)(2,1)} %reshape.24, bf16[1280,1536]{1,0:T(8,128)(2,1)} %param.9), kind=kOutput, calls=%fused_computation.13 | convolution fusion | flops 6039797760 | bytes 17301504 | tf_op jit(solution)/shard_map/dot_general | solution.py:45
  44.5 368.4 %fusion = f32[16,1536]{1,0:T(8,128)S(1)} fusion(f32[1536,1536]{1,0:T(8,128)} %fusion.8), kind=kCustom, calls=%all-reduce-scatter | all-reduce-scatter fusion | flops 3145729 | bytes 9535488
  412.9 1.9 collective-permute-start
  414.8 1.3 collective-permute-start.31
  416.1 1.9 collective-permute-start.1
  418.1 1.3 collective-permute-start.10
  419.4 1.3 collective-permute-start.11
  420.7 1.3 collective-permute-start.12
  422.0 1.3 collective-permute-start.13
  423.3 1.7 collective-permute-done.1
  425.0 12.1 %collective-permute-start.14 = (bf16[16,1536]{1,0:T(8,128)(2,1)S(1)}, bf16[16,1536]{1,0:T(8,128)(2,1)S(1)}, u32[]{:S(2)}, u32[]{:S(2)}) collective-permute-start(bf16[16,1536]{1,0:T(8,128)(2,1)S(1)} %convert.62), channel_id=1, source_target_pairs={{0,15},{1,16},{2,17},{3,18},{4,19},{5,20},{6,21},{7,22},{8,23},{9,... | collective-permute-start | bytes 147464
  437.1 1.3 collective-permute-start.15
  438.4 8.0 %collective-permute-start.16 = (bf16[16,1536]{1,0:T(8,128)(2,1)S(1)}, bf16[16,1536]{1,0:T(8,128)(2,1)S(1)}, u32[]{:S(2)}, u32[]{:S(2)}) collective-permute-start(bf16[16,1536]{1,0:T(8,128)(2,1)S(1)} %convert.62), channel_id=1, source_target_pairs={{0,17},{1,18},{2,19},{3,20},{4,21},{5,22},{6,23},{7,24},{8,25},{9,... | collective-permute-start | bytes 147464
  446.4 7.2 collective-permute-start.17
  453.7 4.0 collective-permute-start.18
  459.0 2.3 collective-permute-start.2
  461.3 3.0 collective-permute-start.20
  464.4 3.8 collective-permute-start.21
  468.2 1.3 collective-permute-start.22
  469.5 1.9 collective-permute-start.23
  471.5 1.9 collective-permute-start.24
  473.4 2.5 collective-permute-start.25
  476.0 1.6 collective-permute-start.26
  477.6 2.2 collective-permute-start.27
  479.9 3.2 collective-permute-start.28
  484.4 4.1 collective-permute-start.3
  488.6 1.9 collective-permute-start.30
  490.5 2.4 collective-permute-start.4
  492.9 1.6 collective-permute-start.5
  494.5 2.9 collective-permute-start.6
  497.5 4.3 collective-permute-start.7
  501.8 1.5 collective-permute-start.8
  503.3 3.4 collective-permute-start.9
  508.1 26.0 %concatenate = bf16[524,1536]{1,0:T(8,128)(2,1)S(1)} concatenate(bf16[12,1536]{1,0:T(8,128)(2,1)S(1)} %collective-permute-done.31, bf16[16,1536]{1,0:T(8,128)(2,1)} %copy-done.22, bf16[16,1536]{1,0:T(8,128)(2,1)} %copy-done.20, bf16[16,1536]{1,0:T(8,128)(2,1)} %copy-done.19, bf16[16,1536]{1,0:T(8,128)(2,1)} %copy-done.18, bf16[16,1536]{1,0:T(8,128)(2,1)} %copy-done.17, ...), dimensions={0} | concatenate | bytes 3268608
  534.0 22.5 %all-gather = bf16[16,12,1536]{2,1,0:T(8,128)(2,1)S(1)} all-gather(bf16[1,12,1536]{2,1,0:T(8,128)(2,1)S(1)} %fusion.4), channel_id=1, replica_groups=mesh['replica'=16,'shard'=8] {'replica'}, dimensions={0}, use_global_device_ids=true | all-gather | bytes 626688 | tf_op jit(solution)/shard_map/all_gather | solution.py:52
  556.7 5.7 fusion.5
  562.4 2.6 stack.2
  565.0 8.0 %all-to-all-start = ((bf16[8,192,1536]{2,1,0:T(8,128)(2,1)}), bf16[8,192,1536]{2,1,0:T(8,128)(2,1)}, u32[]{:S(2)}, u32[]{:S(2)}) async-start(bf16[8,192,1536]{2,1,0:T(8,128)(2,1)} %stack.2), calls=%async_computation | async-start | bytes 9437184 | tf_op jit(solution)/shard_map/all_to_all | solution.py:25
  573.0 1.6 copy.22
  574.6 75.6 %all-to-all-done = bf16[8,192,1536]{2,1,0:T(8,128)(2,1)} async-done(((bf16[8,192,1536]{2,1,0:T(8,128)(2,1)}), bf16[8,192,1536]{2,1,0:T(8,128)(2,1)}, u32[]{:S(2)}, u32[]{:S(2)}) %all-to-all-start) | async-done | bytes 4718624 | tf_op jit(solution)/shard_map/all_to_all | solution.py:25
  650.2 5.5 fusion.2
  655.7 1.6 copy.23
  657.3 55.2 %all-gather.3.cloned.1.call-done = bf16[1536,1536]{1,0:T(8,128)(2,1)} async-done(((bf16[192,1536]{1,0:T(8,128)(2,1)}), bf16[1536,1536]{1,0:T(8,128)(2,1)}) %all-gather.3.cloned.1.call-update) | async-done | bytes 4718608 | tf_op jit(solution)/shard_map/all_gather | solution.py:33
  712.5 10.6 %convolution_convert_fusion = bf16[1280,1536]{1,0:T(8,128)(2,1)} fusion(bf16[1280,1536]{1,0:T(8,128)(2,1)} %param.9, bf16[1536,1536]{1,0:T(8,128)(2,1)} %all-gather.3.cloned.1.call-done), kind=kOutput, calls=%fused_computation | convolution fusion | flops 6041763840 | bytes 12582912 | tf_op jit(solution)/shard_map/dot_general | solution.py:31
  (95 shorter events, 4.0 us)
Async XLA Ops:
  7.2 643.0 %copy-start = (bf16[512,1536]{1,0:T(8,128)(2,1)S(1)}, bf16[512,1536]{1,0:T(8,128)(2,1)}, u32[]{:S(2)}) copy-start(bf16[512,1536]{1,0:T(8,128)(2,1)} %param.15) | copy-start | bytes 4718596
  7.2 705.3 %all-gather.3.cloned.1.call-start = ((), (), s32[]{:S(2)}) async-start(), calls=%async_computation.1 | async-start | bytes 5308416 | tf_op jit(solution)/shard_map/all_gather | solution.py:33
  412.9 9.1 %collective-permute-start = (bf16[16,1536]{1,0:T(8,128)(2,1)S(1)}, bf16[16,1536]{1,0:T(8,128)(2,1)S(1)}, u32[]{:S(2)}, u32[]{:S(2)}) collective-permute-start(bf16[16,1536]{1,0:T(8,128)(2,1)S(1)} %convert.62), channel_id=1, source_target_pairs={{0,1},{1,2},{2,3},{3,4},{4,5},{5,6},{6,7},{7,8},{8,9},{9,10},{10,1... | collective-permute-start | bytes 147464
  414.8 5.8 collective-permute-start.31
  416.1 8.9 %collective-permute-start.1 = (bf16[16,1536]{1,0:T(8,128)(2,1)S(1)}, bf16[16,1536]{1,0:T(8,128)(2,1)S(1)}, u32[]{:S(2)}, u32[]{:S(2)}) collective-permute-start(bf16[16,1536]{1,0:T(8,128)(2,1)S(1)} %convert.62), channel_id=1, source_target_pairs={{0,2},{1,3},{2,4},{3,5},{4,6},{5,7},{6,8},{7,9},{8,10},{9,11},{10,... | collective-permute-start | bytes 147464
  418.1 19.0 %collective-permute-start.10 = (bf16[16,1536]{1,0:T(8,128)(2,1)S(1)}, bf16[16,1536]{1,0:T(8,128)(2,1)S(1)}, u32[]{:S(2)}, u32[]{:S(2)}) collective-permute-start(bf16[16,1536]{1,0:T(8,128)(2,1)S(1)} %convert.62), channel_id=1, source_target_pairs={{0,11},{1,12},{2,13},{3,14},{4,15},{5,16},{6,17},{7,18},{8,19},{9,... | collective-permute-start | bytes 147464
  419.4 19.1 %collective-permute-start.11 = (bf16[16,1536]{1,0:T(8,128)(2,1)S(1)}, bf16[16,1536]{1,0:T(8,128)(2,1)S(1)}, u32[]{:S(2)}, u32[]{:S(2)}) collective-permute-start(bf16[16,1536]{1,0:T(8,128)(2,1)S(1)} %convert.62), channel_id=1, source_target_pairs={{0,12},{1,13},{2,14},{3,15},{4,16},{5,17},{6,18},{7,19},{8,20},{9,... | collective-permute-start | bytes 147464
  420.7 25.8 %collective-permute-start.12 = (bf16[16,1536]{1,0:T(8,128)(2,1)S(1)}, bf16[16,1536]{1,0:T(8,128)(2,1)S(1)}, u32[]{:S(2)}, u32[]{:S(2)}) collective-permute-start(bf16[16,1536]{1,0:T(8,128)(2,1)S(1)} %convert.62), channel_id=1, source_target_pairs={{0,13},{1,14},{2,15},{3,16},{4,17},{5,18},{6,19},{7,20},{8,21},{9,... | collective-permute-start | bytes 147464
  422.0 31.7 %collective-permute-start.13 = (bf16[16,1536]{1,0:T(8,128)(2,1)S(1)}, bf16[16,1536]{1,0:T(8,128)(2,1)S(1)}, u32[]{:S(2)}, u32[]{:S(2)}) collective-permute-start(bf16[16,1536]{1,0:T(8,128)(2,1)S(1)} %convert.62), channel_id=1, source_target_pairs={{0,14},{1,15},{2,16},{3,17},{4,18},{5,19},{6,20},{7,21},{8,22},{9,... | collective-permute-start | bytes 147464
  425.0 32.7 %collective-permute-start.14 = (bf16[16,1536]{1,0:T(8,128)(2,1)S(1)}, bf16[16,1536]{1,0:T(8,128)(2,1)S(1)}, u32[]{:S(2)}, u32[]{:S(2)}) collective-permute-start(bf16[16,1536]{1,0:T(8,128)(2,1)S(1)} %convert.62), channel_id=1, source_target_pairs={{0,15},{1,16},{2,17},{3,18},{4,19},{5,20},{6,21},{7,22},{8,23},{9,... | collective-permute-start | bytes 147464
  437.1 21.9 %collective-permute-start.15 = (bf16[16,1536]{1,0:T(8,128)(2,1)S(1)}, bf16[16,1536]{1,0:T(8,128)(2,1)S(1)}, u32[]{:S(2)}, u32[]{:S(2)}) collective-permute-start(bf16[16,1536]{1,0:T(8,128)(2,1)S(1)} %convert.62), channel_id=1, source_target_pairs={{0,16},{1,17},{2,18},{3,19},{4,20},{5,21},{6,22},{7,23},{8,24},{9,... | collective-permute-start | bytes 147464
  438.4 22.9 %collective-permute-start.16 = (bf16[16,1536]{1,0:T(8,128)(2,1)S(1)}, bf16[16,1536]{1,0:T(8,128)(2,1)S(1)}, u32[]{:S(2)}, u32[]{:S(2)}) collective-permute-start(bf16[16,1536]{1,0:T(8,128)(2,1)S(1)} %convert.62), channel_id=1, source_target_pairs={{0,17},{1,18},{2,19},{3,20},{4,21},{5,22},{6,23},{7,24},{8,25},{9,... | collective-permute-start | bytes 147464
  446.4 60.4 %copy-start.2 = (bf16[16,1536]{1,0:T(8,128)(2,1)}, bf16[16,1536]{1,0:T(8,128)(2,1)S(1)}, u32[]{:S(2)}) copy-start(bf16[16,1536]{1,0:T(8,128)(2,1)S(1)} %collective-permute-done.12) | copy-start | bytes 147460
  446.4 18.0 %collective-permute-start.17 = (bf16[16,1536]{1,0:T(8,128)(2,1)S(1)}, bf16[16,1536]{1,0:T(8,128)(2,1)S(1)}, u32[]{:S(2)}, u32[]{:S(2)}) collective-permute-start(bf16[16,1536]{1,0:T(8,128)(2,1)S(1)} %convert.62), channel_id=1, source_target_pairs={{0,18},{1,19},{2,20},{3,21},{4,22},{5,23},{6,24},{7,25},{8,26},{9,... | collective-permute-start | bytes 147464
  453.7 53.2 %copy-start.3 = (bf16[16,1536]{1,0:T(8,128)(2,1)}, bf16[16,1536]{1,0:T(8,128)(2,1)S(1)}, u32[]{:S(2)}) copy-start(bf16[16,1536]{1,0:T(8,128)(2,1)S(1)} %collective-permute-done.13) | copy-start | bytes 147460
  453.7 14.5 %collective-permute-start.18 = (bf16[16,1536]{1,0:T(8,128)(2,1)S(1)}, bf16[16,1536]{1,0:T(8,128)(2,1)S(1)}, u32[]{:S(2)}, u32[]{:S(2)}) collective-permute-start(bf16[16,1536]{1,0:T(8,128)(2,1)S(1)} %convert.62), channel_id=1, source_target_pairs={{0,19},{1,20},{2,21},{3,22},{4,23},{5,24},{6,25},{7,26},{8,27},{9,... | collective-permute-start | bytes 147464
  457.7 49.1 %copy-start.4 = (bf16[16,1536]{1,0:T(8,128)(2,1)}, bf16[16,1536]{1,0:T(8,128)(2,1)S(1)}, u32[]{:S(2)}) copy-start(bf16[16,1536]{1,0:T(8,128)(2,1)S(1)} %collective-permute-done.14) | copy-start | bytes 147460
  457.7 11.8 %collective-permute-start.19 = (bf16[16,1536]{1,0:T(8,128)(2,1)S(1)}, bf16[16,1536]{1,0:T(8,128)(2,1)S(1)}, u32[]{:S(2)}, u32[]{:S(2)}) collective-permute-start(bf16[16,1536]{1,0:T(8,128)(2,1)S(1)} %convert.62), channel_id=1, source_target_pairs={{0,20},{1,21},{2,22},{3,23},{4,24},{5,25},{6,26},{7,27},{8,28},{9,... | collective-permute-start | bytes 147464
  459.0 47.8 %copy-start.5 = (bf16[16,1536]{1,0:T(8,128)(2,1)}, bf16[16,1536]{1,0:T(8,128)(2,1)S(1)}, u32[]{:S(2)}) copy-start(bf16[16,1536]{1,0:T(8,128)(2,1)S(1)} %collective-permute-done.15) | copy-start | bytes 147460
  459.0 12.4 %collective-permute-start.2 = (bf16[16,1536]{1,0:T(8,128)(2,1)S(1)}, bf16[16,1536]{1,0:T(8,128)(2,1)S(1)}, u32[]{:S(2)}, u32[]{:S(2)}) collective-permute-start(bf16[16,1536]{1,0:T(8,128)(2,1)S(1)} %convert.62), channel_id=1, source_target_pairs={{0,3},{1,4},{2,5},{3,6},{4,7},{5,8},{6,9},{7,10},{8,11},{9,12},{10... | collective-permute-start | bytes 147464
  461.3 45.5 %copy-start.6 = (bf16[16,1536]{1,0:T(8,128)(2,1)}, bf16[16,1536]{1,0:T(8,128)(2,1)S(1)}, u32[]{:S(2)}) copy-start(bf16[16,1536]{1,0:T(8,128)(2,1)S(1)} %collective-permute-done.16) | copy-start | bytes 147460
  461.3 12.1 %collective-permute-start.20 = (bf16[16,1536]{1,0:T(8,128)(2,1)S(1)}, bf16[16,1536]{1,0:T(8,128)(2,1)S(1)}, u32[]{:S(2)}, u32[]{:S(2)}) collective-permute-start(bf16[16,1536]{1,0:T(8,128)(2,1)S(1)} %convert.62), channel_id=1, source_target_pairs={{0,21},{1,22},{2,23},{3,24},{4,25},{5,26},{6,27},{7,28},{8,29},{9,... | collective-permute-start | bytes 147464
  464.4 42.5 %copy-start.7 = (bf16[16,1536]{1,0:T(8,128)(2,1)}, bf16[16,1536]{1,0:T(8,128)(2,1)S(1)}, u32[]{:S(2)}) copy-start(bf16[16,1536]{1,0:T(8,128)(2,1)S(1)} %collective-permute-done.17) | copy-start | bytes 147460
  464.4 11.6 %collective-permute-start.21 = (bf16[16,1536]{1,0:T(8,128)(2,1)S(1)}, bf16[16,1536]{1,0:T(8,128)(2,1)S(1)}, u32[]{:S(2)}, u32[]{:S(2)}) collective-permute-start(bf16[16,1536]{1,0:T(8,128)(2,1)S(1)} %convert.62), channel_id=1, source_target_pairs={{0,22},{1,23},{2,24},{3,25},{4,26},{5,27},{6,28},{7,29},{8,30},{9,... | collective-permute-start | bytes 147464
  468.2 38.7 %copy-start.8 = (bf16[16,1536]{1,0:T(8,128)(2,1)}, bf16[16,1536]{1,0:T(8,128)(2,1)S(1)}, u32[]{:S(2)}) copy-start(bf16[16,1536]{1,0:T(8,128)(2,1)S(1)} %collective-permute-done.18) | copy-start | bytes 147460
  468.2 9.4 %collective-permute-start.22 = (bf16[16,1536]{1,0:T(8,128)(2,1)S(1)}, bf16[16,1536]{1,0:T(8,128)(2,1)S(1)}, u32[]{:S(2)}, u32[]{:S(2)}) collective-permute-start(bf16[16,1536]{1,0:T(8,128)(2,1)S(1)} %convert.62), channel_id=1, source_target_pairs={{0,23},{1,24},{2,25},{3,26},{4,27},{5,28},{6,29},{7,30},{8,31},{9,... | collective-permute-start | bytes 147464
  469.5 37.4 %copy-start.9 = (bf16[16,1536]{1,0:T(8,128)(2,1)}, bf16[16,1536]{1,0:T(8,128)(2,1)S(1)}, u32[]{:S(2)}) copy-start(bf16[16,1536]{1,0:T(8,128)(2,1)S(1)} %collective-permute-done.19) | copy-start | bytes 147460
  469.5 10.3 %collective-permute-start.23 = (bf16[16,1536]{1,0:T(8,128)(2,1)S(1)}, bf16[16,1536]{1,0:T(8,128)(2,1)S(1)}, u32[]{:S(2)}, u32[]{:S(2)}) collective-permute-start(bf16[16,1536]{1,0:T(8,128)(2,1)S(1)} %convert.62), channel_id=1, source_target_pairs={{0,24},{1,25},{2,26},{3,27},{4,28},{5,29},{6,30},{7,31},{8,32},{9,... | collective-permute-start | bytes 147464
  471.5 35.5 %copy-start.10 = (bf16[16,1536]{1,0:T(8,128)(2,1)}, bf16[16,1536]{1,0:T(8,128)(2,1)S(1)}, u32[]{:S(2)}) copy-start(bf16[16,1536]{1,0:T(8,128)(2,1)S(1)} %collective-permute-done.2) | copy-start | bytes 147460
  471.5 11.6 %collective-permute-start.24 = (bf16[16,1536]{1,0:T(8,128)(2,1)S(1)}, bf16[16,1536]{1,0:T(8,128)(2,1)S(1)}, u32[]{:S(2)}, u32[]{:S(2)}) collective-permute-start(bf16[16,1536]{1,0:T(8,128)(2,1)S(1)} %convert.62), channel_id=1, source_target_pairs={{0,25},{1,26},{2,27},{3,28},{4,29},{5,30},{6,31},{7,32},{8,33},{9,... | collective-permute-start | bytes 147464
  473.4 33.5 %copy-start.11 = (bf16[16,1536]{1,0:T(8,128)(2,1)}, bf16[16,1536]{1,0:T(8,128)(2,1)S(1)}, u32[]{:S(2)}) copy-start(bf16[16,1536]{1,0:T(8,128)(2,1)S(1)} %collective-permute-done.20) | copy-start | bytes 147460
  473.4 11.0 %collective-permute-start.25 = (bf16[16,1536]{1,0:T(8,128)(2,1)S(1)}, bf16[16,1536]{1,0:T(8,128)(2,1)S(1)}, u32[]{:S(2)}, u32[]{:S(2)}) collective-permute-start(bf16[16,1536]{1,0:T(8,128)(2,1)S(1)} %convert.62), channel_id=1, source_target_pairs={{0,26},{1,27},{2,28},{3,29},{4,30},{5,31},{6,32},{7,33},{8,34},{9,... | collective-permute-start | bytes 147464
  476.0 31.0 %copy-start.12 = (bf16[16,1536]{1,0:T(8,128)(2,1)}, bf16[16,1536]{1,0:T(8,128)(2,1)S(1)}, u32[]{:S(2)}) copy-start(bf16[16,1536]{1,0:T(8,128)(2,1)S(1)} %collective-permute-done.21) | copy-start | bytes 147460
  476.0 12.6 %collective-permute-start.26 = (bf16[16,1536]{1,0:T(8,128)(2,1)S(1)}, bf16[16,1536]{1,0:T(8,128)(2,1)S(1)}, u32[]{:S(2)}, u32[]{:S(2)}) collective-permute-start(bf16[16,1536]{1,0:T(8,128)(2,1)S(1)} %convert.62), channel_id=1, source_target_pairs={{0,27},{1,28},{2,29},{3,30},{4,31},{5,32},{6,33},{7,34},{8,35},{9,... | collective-permute-start | bytes 147464
  477.6 29.3 %copy-start.13 = (bf16[16,1536]{1,0:T(8,128)(2,1)}, bf16[16,1536]{1,0:T(8,128)(2,1)S(1)}, u32[]{:S(2)}) copy-start(bf16[16,1536]{1,0:T(8,128)(2,1)S(1)} %collective-permute-done.22) | copy-start | bytes 147460
  477.6 12.9 %collective-permute-start.27 = (bf16[16,1536]{1,0:T(8,128)(2,1)S(1)}, bf16[16,1536]{1,0:T(8,128)(2,1)S(1)}, u32[]{:S(2)}, u32[]{:S(2)}) collective-permute-start(bf16[16,1536]{1,0:T(8,128)(2,1)S(1)} %convert.62), channel_id=1, source_target_pairs={{0,28},{1,29},{2,30},{3,31},{4,32},{5,33},{6,34},{7,35},{8,36},{9,... | collective-permute-start | bytes 147464
  479.9 27.1 %copy-start.14 = (bf16[16,1536]{1,0:T(8,128)(2,1)}, bf16[16,1536]{1,0:T(8,128)(2,1)S(1)}, u32[]{:S(2)}) copy-start(bf16[16,1536]{1,0:T(8,128)(2,1)S(1)} %collective-permute-done.23) | copy-start | bytes 147460
  479.9 13.0 %collective-permute-start.28 = (bf16[16,1536]{1,0:T(8,128)(2,1)S(1)}, bf16[16,1536]{1,0:T(8,128)(2,1)S(1)}, u32[]{:S(2)}, u32[]{:S(2)}) collective-permute-start(bf16[16,1536]{1,0:T(8,128)(2,1)S(1)} %convert.62), channel_id=1, source_target_pairs={{0,29},{1,30},{2,31},{3,32},{4,33},{5,34},{6,35},{7,36},{8,37},{9,... | collective-permute-start | bytes 147464
  483.1 11.4 %collective-permute-start.29 = (bf16[16,1536]{1,0:T(8,128)(2,1)S(1)}, bf16[16,1536]{1,0:T(8,128)(2,1)S(1)}, u32[]{:S(2)}, u32[]{:S(2)}) collective-permute-start(bf16[16,1536]{1,0:T(8,128)(2,1)S(1)} %convert.62), channel_id=1, source_target_pairs={{0,30},{1,31},{2,32},{3,33},{4,34},{5,35},{6,36},{7,37},{8,38},{9,... | collective-permute-start | bytes 147464
  484.4 13.0 %collective-permute-start.3 = (bf16[16,1536]{1,0:T(8,128)(2,1)S(1)}, bf16[16,1536]{1,0:T(8,128)(2,1)S(1)}, u32[]{:S(2)}, u32[]{:S(2)}) collective-permute-start(bf16[16,1536]{1,0:T(8,128)(2,1)S(1)} %convert.62), channel_id=1, source_target_pairs={{0,4},{1,5},{2,6},{3,7},{4,8},{5,9},{6,10},{7,11},{8,12},{9,13},{1... | collective-permute-start | bytes 147464
  488.6 13.2 %collective-permute-start.30 = (bf16[16,1536]{1,0:T(8,128)(2,1)S(1)}, bf16[16,1536]{1,0:T(8,128)(2,1)S(1)}, u32[]{:S(2)}, u32[]{:S(2)}) collective-permute-start(bf16[16,1536]{1,0:T(8,128)(2,1)S(1)} %convert.62), channel_id=1, source_target_pairs={{0,31},{1,32},{2,33},{3,34},{4,35},{5,36},{6,37},{7,38},{8,39},{9,... | collective-permute-start | bytes 147464
  490.5 12.8 %collective-permute-start.4 = (bf16[16,1536]{1,0:T(8,128)(2,1)S(1)}, bf16[16,1536]{1,0:T(8,128)(2,1)S(1)}, u32[]{:S(2)}, u32[]{:S(2)}) collective-permute-start(bf16[16,1536]{1,0:T(8,128)(2,1)S(1)} %convert.62), channel_id=1, source_target_pairs={{0,5},{1,6},{2,7},{3,8},{4,9},{5,10},{6,11},{7,12},{8,13},{9,14},{... | collective-permute-start | bytes 147464
  492.9 13.9 %collective-permute-start.5 = (bf16[16,1536]{1,0:T(8,128)(2,1)S(1)}, bf16[16,1536]{1,0:T(8,128)(2,1)S(1)}, u32[]{:S(2)}, u32[]{:S(2)}) collective-permute-start(bf16[16,1536]{1,0:T(8,128)(2,1)S(1)} %convert.62), channel_id=1, source_target_pairs={{0,6},{1,7},{2,8},{3,9},{4,10},{5,11},{6,12},{7,13},{8,14},{9,15},... | collective-permute-start | bytes 147464
  494.5 12.3 %collective-permute-start.6 = (bf16[16,1536]{1,0:T(8,128)(2,1)S(1)}, bf16[16,1536]{1,0:T(8,128)(2,1)S(1)}, u32[]{:S(2)}, u32[]{:S(2)}) collective-permute-start(bf16[16,1536]{1,0:T(8,128)(2,1)S(1)} %convert.62), channel_id=1, source_target_pairs={{0,7},{1,8},{2,9},{3,10},{4,11},{5,12},{6,13},{7,14},{8,15},{9,16}... | collective-permute-start | bytes 147464
  497.5 9.3 %collective-permute-start.7 = (bf16[16,1536]{1,0:T(8,128)(2,1)S(1)}, bf16[16,1536]{1,0:T(8,128)(2,1)S(1)}, u32[]{:S(2)}, u32[]{:S(2)}) collective-permute-start(bf16[16,1536]{1,0:T(8,128)(2,1)S(1)} %convert.62), channel_id=1, source_target_pairs={{0,8},{1,9},{2,10},{3,11},{4,12},{5,13},{6,14},{7,15},{8,16},{9,17... | collective-permute-start | bytes 147464
  501.8 5.0 collective-permute-start.8
  503.3 4.7 collective-permute-start.9
  565.0 85.1 %all-to-all-start = ((bf16[8,192,1536]{2,1,0:T(8,128)(2,1)}), bf16[8,192,1536]{2,1,0:T(8,128)(2,1)}, u32[]{:S(2)}, u32[]{:S(2)}) async-start(bf16[8,192,1536]{2,1,0:T(8,128)(2,1)} %stack.2), calls=%async_computation | async-start | bytes 9437184 | tf_op jit(solution)/shard_map/all_to_all | solution.py:25
  (14 other events, 136.8 us)
Sparse Core Ops, SparseCore 0:
  562.5 149.8 all-gather.2
